TPU v7x, 32 devices: a whole 2x2x4 slice. The times are simulated.
32 devices in a mesh: seq: 8 (over y, x, core), tensor: 4 (over z).
Axes of the slice: x: 2, y: 2, z: 4, core: 2. Of those that a mesh axis runs over, the one named last changes fastest.
Arguments:
- hidden: bfloat16 [8192, 3072], P('seq', 'tensor'), may hold values from -6 to 6
- norm_gain: float32 [3072], replicated, may hold values from 0.1 to 1.9
- query_weight: bfloat16 [3072, 4096], P(None, 'tensor'), may hold values from -0.25 to 0.25
- key_weight: bfloat16 [3072, 4096], P(None, 'tensor'), may hold values from -2 to 2
- value_weight: bfloat16 [3072, 4096], P(None, 'tensor'), may hold values from -0.109375 to 0.109375
- output_weight: bfloat16 [4096, 3072], P('tensor'), may hold values from -1.25 to 1.25
- final_gain: float32 [3072], replicated, may hold values from 0.1 to 1.9
- reward_weight: float32 [3072], replicated, may hold values from -6 to 6
- token_ids: int32 [8192], P(('seq', 'tensor')), may hold values from 0 to 255999, as said below
- index_samples: float32 [8, 8, 8192], P(None, None, ('seq', 'tensor')), may hold values from -6 to 6
- feat_weight: float32 [3072, 256], replicated, may hold values from -0.109375 to 0.109375
- index_weight: float32 [8, 256], replicated, may hold values from -2 to 2
- first_bias: float32 [256], replicated, may hold values from -3 to 3
- middle_weight: float32 [256, 256], replicated, may hold values from -0.375 to 0.375
- second_bias: float32 [256], replicated, may hold values from -3 to 3
- head_weight: float32 [256, 8], replicated, may hold values from -0.375 to 0.375
- pair_ids: int32 [8, 2], replicated, may hold values from 0 to 15, all different within a row
Outputs:
- features: bfloat16 [8192, 3072], P(('seq', 'tensor'))
- pair_margin: float32 [8, 8], replicated
- grad_feature: float32 [3072, 256], P(('seq', 'tensor'))
- grad_index: float32 [8, 256], replicated
- grad_first: float32 [256], replicated
- grad_middle: float32 [256, 256], replicated
- grad_second: float32 [256], replicated
- grad_head: float32 [256, 8], replicated
Inputs may be any that keep to these rules, and one draw needn't show every extreme that they name: `token_ids`: in each response of 512 positions the positions before its last valid one hold ids from 2 to 255999, the last valid one holds 1 and the positions after it hold 0; every response has at least 128 valid tokens and at least one 0; the first position of the first response holds 255999. `pair_ids`: each row names two different responses, chosen first; every response stands in exactly one pair.
All inputs are finite; a program needn't handle non-finite values.
Results may differ from a plain program's by a relative error of at most 0.012.
The roundings to bfloat16 on the way count: a program that leaves them out, or rounds other values in their place, can miss the bound.
Values may be sent and summed in bfloat16 or wider, within the bound.
A program may use at most 128 MiB of HBM per device.

v0:
```python
import jax
import jax.numpy as jnp
from jax import lax
from jax.sharding import PartitionSpec as P

HEAD_DIM = 256
RESP_LEN = 512


norm_eps = 1e-06
rope_base = 10000.0
gelu_coef = 0.044715
gelu_root = 0.7978845608028654
masked_score = -1e30


def rms_scale(rows, gain):
    mean_square = jnp.mean(rows * rows, axis=-1, keepdims=True)
    return rows * lax.rsqrt(mean_square + norm_eps) * (1.0 + gain)


def rotate_pairs(entries, positions):
    half_dim = entries.shape[-1] // 2
    freqs = rope_base ** (-(jnp.arange(half_dim, dtype=jnp.float32) * 2.0) / entries.shape[-1])
    angles = positions.astype(jnp.float32)[:, None] * freqs[None, :]
    cosine = jnp.cos(angles)[:, None, :]
    sine = jnp.sin(angles)[:, None, :]
    first_half = entries[..., :half_dim]
    second_half = entries[..., half_dim:]
    return jnp.concatenate(
        [first_half * cosine - second_half * sine, second_half * cosine + first_half * sine],
        axis=-1,
    )


def gelu_tanh(inputs):
    return (
        0.5 * inputs * (1.0 + jnp.tanh(gelu_root * (inputs + gelu_coef * inputs * inputs * inputs)))
    )


def gelu_slope(inputs):
    tangent = jnp.tanh(gelu_root * (inputs + gelu_coef * inputs * inputs * inputs))
    inner_slope = gelu_root * (1.0 + 3.0 * gelu_coef * inputs * inputs)
    return 0.5 * (1.0 + tangent) + 0.5 * inputs * (1.0 - tangent * tangent) * inner_slope


def shards(
    hidden,
    norm_gain,
    query_weight,
    key_weight,
    value_weight,
    output_weight,
    final_gain,
    reward_weight,
    token_ids,
    index_samples,
    feat_weight,
    index_weight,
    first_bias,
    middle_weight,
    second_bias,
    head_weight,
    pair_ids,
):
    tp_count = lax.axis_size("tensor")
    tp_index = lax.axis_index("tensor")
    seq_index = lax.axis_index("seq")
    whole_rows = lax.all_gather(hidden, "tensor", axis=1, tiled=True)
    tok_seq = whole_rows.shape[0]
    width = whole_rows.shape[1]
    local_heads = query_weight.shape[1] // HEAD_DIM
    local_resp = tok_seq // RESP_LEN
    normed = rms_scale(whole_rows.astype(jnp.float32), norm_gain).astype(jnp.bfloat16)
    positions = jnp.arange(RESP_LEN, dtype=jnp.int32)
    causal = positions[None, :] <= positions[:, None]
    head_shape = (local_resp, RESP_LEN, local_heads, HEAD_DIM)
    queries = jnp.dot(normed, query_weight, preferred_element_type=jnp.float32).reshape(head_shape)
    queries = rotate_pairs(queries, positions).astype(jnp.bfloat16)
    key_rows = jnp.dot(normed, key_weight, preferred_element_type=jnp.float32).reshape(head_shape)
    key_rows = rotate_pairs(key_rows, positions).astype(jnp.bfloat16)
    value_rows = (
        jnp.dot(normed, value_weight, preferred_element_type=jnp.float32)
        .astype(jnp.bfloat16)
        .reshape(head_shape)
    )
    scores = jnp.einsum(
        "rqhd,rkhd->rhqk", queries, key_rows, preferred_element_type=jnp.float32
    ) * HEAD_DIM ** (-0.5)
    scores = jnp.where(causal[None, None, :, :], scores, masked_score)
    highest = jnp.max(scores, axis=-1, keepdims=True)
    weights = jnp.exp(scores - highest)
    probs = (weights / jnp.sum(weights, axis=-1, keepdims=True)).astype(jnp.bfloat16)
    attended = jnp.einsum(
        "rhqk,rkhd->rqhd", probs, value_rows, preferred_element_type=jnp.float32
    ).astype(jnp.bfloat16)
    attended = attended.reshape(tok_seq, local_heads * HEAD_DIM)
    partial_out = jnp.dot(attended, output_weight, preferred_element_type=jnp.float32)
    mixed = lax.psum_scatter(partial_out, "tensor", scatter_dimension=1, tiled=True)
    local_width = mixed.shape[1]
    summed = hidden.astype(jnp.float32) + mixed
    square_sums = lax.psum(jnp.sum(summed * summed, axis=1), "tensor")
    gain_part = lax.dynamic_slice_in_dim(final_gain, tp_index * local_width, local_width, 0)
    local_feat = (
        summed * lax.rsqrt(square_sums[:, None] / width + norm_eps) * (1.0 + gain_part)
    ).astype(jnp.bfloat16)
    features = lax.all_to_all(local_feat, "tensor", split_axis=0, concat_axis=1, tiled=True)
    feat32 = features.astype(jnp.float32)
    tok_epi = feat32.shape[0]
    base = jnp.dot(feat32, reward_weight, precision=lax.Precision.HIGHEST)
    feat_part = jnp.dot(feat32, feat_weight, precision=lax.Precision.HIGHEST)
    index_part = jnp.einsum(
        "sit,ie->ste", index_samples, index_weight, precision=lax.Precision.HIGHEST
    )
    first_pre = feat_part[None, :, :] + index_part + first_bias
    first_act = gelu_tanh(first_pre)
    second_pre = (
        jnp.einsum("ste,ef->stf", first_act, middle_weight, precision=lax.Precision.HIGHEST)
        + second_bias
    )
    second_act = gelu_tanh(second_pre)
    head_out = jnp.einsum("ste,ei->sti", second_act, head_weight, precision=lax.Precision.HIGHEST)
    epinet_out = jnp.einsum("sti,sit->st", head_out, index_samples, precision=lax.Precision.HIGHEST)
    resp_total = 2 * pair_ids.shape[0]
    first_token = (seq_index * tp_count + tp_index) * tok_epi
    token_pos = first_token + jnp.arange(tok_epi, dtype=jnp.int32)
    owner = token_pos // RESP_LEN
    slot_ids = jnp.arange(resp_total, dtype=jnp.int32)
    owner_table = (owner[:, None] == slot_ids[None, :]).astype(jnp.float32)
    valid = (token_ids != 0).astype(jnp.float32)
    part_totals = jnp.dot(
        (base[None, :] + epinet_out) * valid[None, :], owner_table, precision=lax.Precision.HIGHEST
    )
    part_counts = jnp.dot(valid, owner_table, precision=lax.Precision.HIGHEST)
    totals, counts = lax.psum((part_totals, part_counts), ("seq", "tensor"))
    means = totals / counts[None, :]
    sign_table = (pair_ids[:, 0:1] == slot_ids[None, :]).astype(jnp.float32) - (
        pair_ids[:, 1:2] == slot_ids[None, :]
    ).astype(jnp.float32)
    margin = jnp.dot(means, sign_table.T, precision=lax.Precision.HIGHEST)
    pair_margin = margin.T
    margin_grad = -jax.nn.sigmoid(-margin)
    mean_grad = jnp.dot(margin_grad, sign_table, precision=lax.Precision.HIGHEST) / counts[None, :]
    reward_grad = (
        jnp.dot(mean_grad, owner_table.T, precision=lax.Precision.HIGHEST) * valid[None, :]
    )
    out_grad = jnp.einsum("st,sit->sti", reward_grad, index_samples)
    grad_head = jnp.einsum("ste,sti->ei", second_act, out_grad, precision=lax.Precision.HIGHEST)
    second_grad = jnp.einsum(
        "sti,ei->ste", out_grad, head_weight, precision=lax.Precision.HIGHEST
    ) * gelu_slope(second_pre)
    grad_second = jnp.sum(second_grad, axis=(0, 1))
    grad_middle = jnp.einsum("ste,stf->ef", first_act, second_grad, precision=lax.Precision.HIGHEST)
    first_grad = jnp.einsum(
        "stf,ef->ste", second_grad, middle_weight, precision=lax.Precision.HIGHEST
    ) * gelu_slope(first_pre)
    grad_first = jnp.sum(first_grad, axis=(0, 1))
    grad_index = jnp.einsum(
        "sit,ste->ie", index_samples, first_grad, precision=lax.Precision.HIGHEST
    )
    feat_grad = jnp.sum(first_grad, axis=0)
    grad_feature = lax.psum_scatter(
        jnp.einsum("td,te->de", feat32, feat_grad, precision=lax.Precision.HIGHEST),
        ("seq", "tensor"),
        scatter_dimension=0,
        tiled=True,
    )
    summed_grads = lax.psum(
        (grad_index, grad_first, grad_middle, grad_second, grad_head), ("seq", "tensor")
    )
    return (
        features,
        pair_margin,
        grad_feature,
        summed_grads[0],
        summed_grads[1],
        summed_grads[2],
        summed_grads[3],
        summed_grads[4],
    )


def solution(mesh):
    return jax.shard_map(
        shards,
        mesh=mesh,
        in_specs=(
            P("seq", "tensor"),
            P(),
            P(None, "tensor"),
            P(None, "tensor"),
            P(None, "tensor"),
            P("tensor", None),
            P(),
            P(),
            P(("seq", "tensor")),
            P(None, None, ("seq", "tensor")),
            P(),
            P(),
            P(),
            P(),
            P(),
            P(),
            P(),
        ),
        out_specs=(
            P(("seq", "tensor"), None),
            P(),
            P(("seq", "tensor"), None),
            P(),
            P(),
            P(),
            P(),
            P(),
        ),
        check_vma=False,
    )
```

profile of v0, /device:TPU:9, one launch (start us, length us, event | category | flops | bytes accessed | tf_op | source)
XLA Modules:
  0.0 793.9 jit_solution(2931273031737406126)
XLA Ops:
  11.2 112.1 %all-gather.2.cloned.1.call-done = bf16[1024,3072]{1,0:T(8,128)(2,1)} async-done(((bf16[1024,768]{1,0:T(8,128)(2,1)}), bf16[1024,3072]{1,0:T(8,128)(2,1)}) %all-gather.2.cloned.1.call-update) | async-done | bytes 6291472 | tf_op jit(solution)/shard_map/all_gather | solution.py:70
  123.3 4.2 fusion.1
  127.9 9.9 %convolution_convert_fusion = bf16[1024,1024]{1,0:T(8,128)(2,1)} fusion(bf16[3072,1024]{1,0:T(8,128)(2,1)} %param.21, bf16[1024,3072]{1,0:T(8,128)(2,1)S(1)} %copy-done.2, f32[3072]{0:T(1024)S(1)} %broadcast_add_fusion, f32[1024]{0:T(1024)S(1)} %add_rsqrt_fusion.1), kind=kOutput, calls=%fused_computation.51 | convolution fusion | flops 6456082432 | bytes 14696448 | tf_op jit(solution)/shard_map/dot_general | solution.py:84
  137.8 4.5 reshape.148
  142.4 12.1 %fusion.86 = f32[1024,1024]{1,0:T(8,128)} fusion(bf16[3072,1024]{1,0:T(8,128)(2,1)} %param.20, bf16[1024,3072]{1,0:T(8,128)(2,1)} %all-gather.2.cloned.1.call-done, f32[3072]{0:T(1024)S(1)} %broadcast_add_fusion, f32[1024]{0:T(1024)S(1)} %add_rsqrt_fusion.1), kind=kOutput, calls=%fused_computation.132 | convolution fusion | flops 6455033856 | bytes 16793600 | tf_op jit(solution)/shard_map/dot_general | solution.py:81
  154.5 5.6 reshape.150
  160.1 12.1 %fusion.88 = f32[1024,1024]{1,0:T(8,128)} fusion(bf16[3072,1024]{1,0:T(8,128)(2,1)} %param.19, bf16[1024,3072]{1,0:T(8,128)(2,1)} %all-gather.2.cloned.1.call-done, f32[3072]{0:T(1024)S(1)} %broadcast_add_fusion, f32[1024]{0:T(1024)S(1)} %add_rsqrt_fusion.1), kind=kOutput, calls=%fused_computation.133 | convolution fusion | flops 6455033856 | bytes 16793600 | tf_op jit(solution)/shard_map/dot_general | solution.py:79
  172.2 6.1 reshape.149
  178.3 4.1 fusion.93
  185.1 5.6 fusion.95
  190.7 6.1 convert_bitcast_fusion
  196.8 4.2 copy.40
  201.0 2.1 copy.56
  203.1 12.3 %fusion.97 = f32[1024,3072]{1,0:T(8,128)} fusion(bf16[1024,1024]{1,0:T(8,128)(2,1)S(1)} %bitcast.76, bf16[1024,3072]{1,0:T(8,128)(2,1)} %param.22), kind=kOutput, calls=%fused_computation.140 | convolution fusion | flops 6442450944 | bytes 20971520 | tf_op jit(solution)/shard_map/dot_general | solution.py:99
  216.2 212.3 %reduce-scatter.3.cloned.1.call-done = f32[1024,768]{1,0:T(8,128)} async-done(((f32[1024,3072]{1,0:T(8,128)}), f32[1024,768]{1,0:T(8,128)}) %reduce-scatter.3.cloned.1.call-update) | async-done | bytes 3145744 | tf_op jit(solution)/shard_map/reduce_scatter | solution.py:100
  428.5 2.8 multiply_reduce_fusion
  431.4 8.0 %psum.56 = f32[1024]{0:T(1024)S(1)} all-reduce(f32[1024]{0:T(1024)S(1)} %multiply_reduce_fusion), channel_id=1, replica_groups=mesh['seq'=8,'tensor'=4] {'tensor'}, use_global_device_ids=true, to_apply=%region_5.6 | all-reduce | flops 1024 | bytes 8192 | tf_op jit(solution)/shard_map/psum | solution.py:103
  439.3 4.0 multiply_convert_fusion
  443.3 6.4 all-to-all-start
  450.1 31.1 %all-to-all-done = bf16[4,256,768]{2,1,0:T(8,128)(2,1)} async-done(((bf16[4,256,768]{2,1,0:T(8,128)(2,1)}), bf16[4,256,768]{2,1,0:T(8,128)(2,1)}, u32[]{:S(2)}, u32[]{:S(2)}) %all-to-all-start) | async-done | bytes 1572896 | tf_op jit(solution)/shard_map/all_to_all | solution.py:108
  486.0 2.0 add_add_fusion
  488.0 2.3 fusion.34
  490.4 2.5 fusion.33
  493.2 44.3 %all-reduce.1 = (f32[8,16]{1,0:T(8,128)S(1)}, f32[16]{0:T(128)S(1)}) all-reduce(f32[8,16]{1,0:T(8,128)S(1)} %fusion.37, f32[16]{0:T(128)S(1)} %convolution_bitcast_fusion.3), channel_id=1, replica_groups=mesh['seq'=8,'tensor'=4] {'seq','tensor'}, use_global_device_ids=true, to_apply=%region_6.7 | all-reduce | flops 144 | bytes 1152 | tf_op jit(solution)/shard_map/psum | solution.py:136
  538.1 4.9 fusion.96
  544.4 4.6 convolution_bitcast_fusion
  549.1 6.6 fusion.91
  556.0 4.8 fusion.100
  561.5 2.8 convolution_bitcast_fusion.2
  566.1 39.3 %all-reduce = (f32[8,256]{1,0:T(8,128)}, f32[256]{0:T(256)}, f32[256]{0:T(256)}, f32[256,8]{0,1:T(8,128)}) all-reduce(f32[8,256]{1,0:T(8,128)S(1)} %convolution_bitcast_fusion.2, f32[256]{0:T(256)S(1)} %get-tuple-element.24, f32[256]{0:T(256)S(1)} %get-tuple-element.51, ...), channel_id=1, replica_groups=mesh['seq'=8,'tensor'=4] {'seq','tensor'}, use_global_device_ids=true, to_apply=%region_10.11 | all-reduce | flops 4608 | bytes 36864 | tf_op jit(solution)/shard_map/psum | solution.py:169
  605.4 73.4 %all-reduce.4.cloned.1.call-done = f32[256,256]{1,0:T(8,128)} async-done(((f32[256,256]{1,0:T(8,128)}), f32[256,256]{1,0:T(8,128)}) %all-reduce.4.cloned.1.call-update) | async-done | bytes 262160 | tf_op jit(solution)/shard_map/psum | solution.py:169
  678.8 106.5 %reduce-scatter.5.cloned.1.call-done = f32[96,256]{1,0:T(8,128)} async-done(((f32[3072,256]{1,0:T(8,128)}), f32[96,256]{1,0:T(8,128)}) %reduce-scatter.5.cloned.1.call-update) | async-done | bytes 98320 | tf_op jit(solution)/shard_map/reduce_scatter | solution.py:163
  (73 shorter events, 19.6 us)
Async XLA Ops:
  7.2 477.0 %copy-start = (f32[3072,256]{1,0:T(8,128)S(1)}, f32[3072,256]{1,0:T(8,128)}, u32[]{:S(2)}) copy-start(f32[3072,256]{1,0:T(8,128)} %param.27) | copy-start | bytes 9437188
  7.2 116.1 %all-gather.2.cloned.1.call-start = ((), (), s32[]{:S(2)}) async-start(), calls=%async_computation.3 | async-start | bytes 7864320 | tf_op jit(solution)/shard_map/all_gather | solution.py:70
  7.9 420.6 %reduce-scatter.3.cloned.1.call-start = ((), (), s32[]{:S(2)}) async-start(), calls=%async_computation.4 | async-start | bytes 15728640 | tf_op jit(solution)/shard_map/reduce_scatter | solution.py:100
  123.3 4.6 copy-start.2
  178.3 4.2 copy-start.6
  183.7 1.3 copy-start.8
  185.0 5.6 copy-start.3
  443.3 6.6 copy-start.12
  443.3 6.8 copy-start.13
  443.3 37.9 %all-to-all-start = ((bf16[4,256,768]{2,1,0:T(8,128)(2,1)}), bf16[4,256,768]{2,1,0:T(8,128)(2,1)}, u32[]{:S(2)}, u32[]{:S(2)}) async-start(bf16[4,256,768]{2,1,0:T(8,128)(2,1)} %bitcast.75), calls=%async_computation.1 | async-start | bytes 3145728 | tf_op jit(solution)/shard_map/all_to_all | solution.py:108
  449.7 33.1 %copy-start.9 = (f32[3072]{0:T(1024)S(1)}, f32[3072]{0:T(1024)}, u32[]{:S(2)}) copy-start(f32[3072]{0:T(1024)} %param.24) | copy-start | bytes 36868
  449.7 229.1 %all-reduce.4.cloned.1.call-start = ((), (), s32[]{:S(2)}) async-start(), calls=%async_computation.6 | async-start | bytes 524288 | tf_op jit(solution)/shard_map/psum | solution.py:169
  482.8 3.2 copy-start.1
  484.1 1.8 copy-start.7
  484.2 1.8 copy-start.10
  484.2 1.8 copy-start.11
  486.0 2.0 copy-start.14
  488.0 2.4 copy-start.4
  488.0 2.4 copy-start.15
  488.0 2.4 copy-start.16
  490.4 2.6 copy-start.17
  538.1 6.3 copy-start.5
  543.0 1.4 copy-start.19
  555.7 229.6 %reduce-scatter.5.cloned.1.call-start = ((), (), s32[]{:S(2)}) async-start(), calls=%async_computation.5 | async-start | bytes 3244032 | tf_op jit(solution)/shard_map/reduce_scatter | solution.py:163
  561.5 2.8 copy-start.18
Sparse Core Ops, SparseCore 0:
  9.6 113.6 all-gather.1
  215.6 212.9 reduce-scatter.2
  555.8 122.8 all-reduce.3
  684.6 100.6 reduce-scatter.4
where the time goes:
time: 806 us; the launch traced here: 794 us
  waiting for transfers between devices  536 us (67%)
  blocking collectives  91.5 us (11%)
  matrix products  90.4 us (11%)
  local copies, waits for them, and re-layouts  32.5 us (4%)
  other arithmetic  22 us (3%)
  between operations  14.6 us (2%)
    reduce_scatter x1, waiting for transfers between devices, shards(): lax.psum_scatter(partial_out, 'tensor', scatter_dimension=1, tiled=True)  212 us
    all_gather x1, waiting for transfers between devices, shards(): whole_rows = lax.all_gather(hidden, 'tensor', axis=1, tiled=True)  112 us
    reduce_scatter x1, waiting for transfers between devices, shards(): lax.psum_scatter(jnp.einsum('td,te->de', feat32, feat_grad, precision=lax...  107 us
    psum x1, waiting for transfers between devices, shards(): lax.psum((grad_index, grad_first, grad_middle, grad_second, grad_head), (...  73.4 us
    psum x1, blocking collectives, shards(): totals, counts = lax.psum((part_totals, part_counts), ('seq', 'tensor'))  44.3 us
    psum x1, blocking collectives, shards(): lax.psum((grad_index, grad_first, grad_middle, grad_second, grad_head), (...  39.3 us
    all_to_all x1, waiting for transfers between devices, shards(): lax.all_to_all(local_feat, 'tensor', split_axis=0, concat_axis=1, tiled=T...  31.1 us
  transfers between devices with their start and end apart: 5, of which 5 were waited for; matrix products, arithmetic and copies ran while one was open for 2% of the time, Pallas kernels for 0%

commit v1 on v0

v1 whole, which is shorter than its diff:
```python
import functools

import jax
import jax.numpy as jnp
from jax import lax
from jax.experimental import pallas as pl
from jax.experimental.pallas import tpu as pltpu
from jax.sharding import PartitionSpec as P

HEAD_DIM = 256
RESP_LEN = 512
MESH = pl.DeviceIdType.MESH

norm_eps = 1e-06
rope_base = 10000.0
gelu_coef = 0.044715
gelu_root = 0.7978845608028654
masked_score = -1e30


def gelu_tanh(inputs):
    return (
        0.5 * inputs * (1.0 + jnp.tanh(gelu_root * (inputs + gelu_coef * inputs * inputs * inputs)))
    )


def gelu_slope(inputs):
    tangent = jnp.tanh(gelu_root * (inputs + gelu_coef * inputs * inputs * inputs))
    inner_slope = gelu_root * (1.0 + 3.0 * gelu_coef * inputs * inputs)
    return 0.5 * (1.0 + tangent) + 0.5 * inputs * (1.0 - tangent * tangent) * inner_slope


def attention_kernel(
    x_ref, gain_ref, wq_ref, wk_ref, wv_ref, cos_ref, sin_ref, out_ref, normed_ref
):
    parts, rows, width = x_ref.shape
    step = 64

    @pl.when(pl.program_id(0) == 0)
    def _():
        def body(i, carry):
            at = pl.ds(pl.multiple_of(i * step, step), step)
            total = jnp.zeros((step, 1), jnp.float32)
            for p in range(parts):
                x = x_ref[p, at, :].astype(jnp.float32)
                total = total + jnp.sum(x * x, axis=-1, keepdims=True)
            scale = lax.rsqrt(total / (parts * width) + norm_eps)
            for p in range(parts):
                x = x_ref[p, at, :].astype(jnp.float32)
                gain = 1.0 + gain_ref[p : p + 1, :]
                normed_ref[at, p * width : (p + 1) * width] = (x * scale * gain).astype(
                    jnp.bfloat16
                )
            return carry

        lax.fori_loop(0, rows // step, body, 0)

    normed = normed_ref[...]
    cosine = cos_ref[...]
    sine = sin_ref[...]
    half = HEAD_DIM // 2

    def rotated(w_ref):
        full = jnp.dot(normed, w_ref[...], preferred_element_type=jnp.float32)
        a = full[:, :half]
        b = full[:, half:]
        return jnp.concatenate([a * cosine - b * sine, b * cosine + a * sine], axis=-1).astype(
            jnp.bfloat16
        )

    queries = rotated(wq_ref)
    keys = rotated(wk_ref)
    values = jnp.dot(normed, wv_ref[...], preferred_element_type=jnp.float32).astype(jnp.bfloat16)
    scores = lax.dot_general(
        queries, keys, (((1,), (1,)), ((), ())), preferred_element_type=jnp.float32
    ) * HEAD_DIM ** (-0.5)
    q_pos = lax.broadcasted_iota(jnp.int32, scores.shape, 0)
    k_pos = lax.broadcasted_iota(jnp.int32, scores.shape, 1)
    scores = jnp.where(k_pos <= q_pos, scores, masked_score)
    highest = jnp.max(scores, axis=-1, keepdims=True)
    weights = jnp.exp(scores - highest)
    probs = (weights / jnp.sum(weights, axis=-1, keepdims=True)).astype(jnp.bfloat16)
    out_ref[...] = jnp.dot(probs, values, preferred_element_type=jnp.float32).astype(jnp.bfloat16)


def attend(x, gain, wq, wk, wv, cosine, sine):
    parts, rows, width = x.shape
    depth = parts * width
    heads = wq.shape[1] // HEAD_DIM
    weight = pl.BlockSpec((depth, HEAD_DIM), lambda h: (0, h))
    table = pl.BlockSpec((rows, HEAD_DIM // 2), lambda h: (0, 0))
    return pl.pallas_call(
        attention_kernel,
        grid=(heads,),
        out_shape=jax.ShapeDtypeStruct((rows, heads * HEAD_DIM), jnp.bfloat16),
        in_specs=[
            pl.BlockSpec((parts, rows, width), lambda h: (0, 0, 0)),
            pl.BlockSpec((parts, width), lambda h: (0, 0)),
            weight,
            weight,
            weight,
            table,
            table,
        ],
        out_specs=pl.BlockSpec((rows, HEAD_DIM), lambda h: (0, h)),
        scratch_shapes=[pltpu.VMEM((rows, depth), jnp.bfloat16)],
        compiler_params=pltpu.CompilerParams(vmem_limit_bytes=48 * 1024 * 1024),
        cost_estimate=pl.CostEstimate(
            flops=2 * rows * depth * HEAD_DIM * heads * 3 + 4 * rows * rows * HEAD_DIM * heads,
            bytes_accessed=rows * depth * 2 + 3 * depth * HEAD_DIM * heads * 2,
            transcendentals=rows * rows * heads,
        ),
    )(x, gain, wq, wk, wv, cosine, sine)


def push(axis, count, sources, targets, send_sems, recv_sems):
    me = lax.axis_index(axis)
    copies = []
    for k in range(1, count):
        peer = lax.rem(me + k, count)
        for j, (source, target) in enumerate(zip(sources, targets)):
            copy = pltpu.make_async_remote_copy(
                src_ref=source(peer),
                dst_ref=target.at[k],
                send_sem=send_sems.at[j, k],
                recv_sem=recv_sems.at[j, k],
                device_id={axis: peer},
                device_id_type=MESH,
            )
            copy.start()
            copies.append(copy)
    return copies


def greet(seq_count, tp_count):
    barrier = pltpu.get_barrier_semaphore()
    for axis, count in (("seq", seq_count), ("tensor", tp_count)):
        me = lax.axis_index(axis)
        for k in range(1, count):
            pl.semaphore_signal(
                barrier, inc=1, device_id={axis: lax.rem(me + k, count)}, device_id_type=MESH
            )
    pl.semaphore_wait(barrier, seq_count + tp_count - 2)


def ordered_sum(axis, count, slots):
    me = lax.axis_index(axis)
    total = slots[lax.rem(me + count, count)]
    for origin in range(1, count):
        total = total + slots[lax.rem(me - origin + count, count)]
    return total


def totals_kernel(
    seq_count, tp_count, part_ref, out_ref, first, mid, second, send1, recv1, send2, recv2
):
    greet(seq_count, tp_count)
    copies = push("seq", seq_count, [lambda p: part_ref], [first], send1, recv1)
    first[0] = part_ref[...]
    for copy in copies:
        copy.wait()
    mid[...] = ordered_sum("seq", seq_count, first)
    copies = push("tensor", tp_count, [lambda p: mid], [second], send2, recv2)
    second[0] = mid[...]
    for copy in copies:
        copy.wait()
    out_ref[...] = ordered_sum("tensor", tp_count, second)


def sum_everywhere(part, seq_count, tp_count):
    rows, lanes = part.shape
    vmem = pl.BlockSpec(memory_space=pltpu.VMEM)
    return pl.pallas_call(
        functools.partial(totals_kernel, seq_count, tp_count),
        out_shape=jax.ShapeDtypeStruct(part.shape, jnp.float32),
        in_specs=[vmem],
        out_specs=vmem,
        scratch_shapes=[
            pltpu.VMEM((seq_count, rows, lanes), jnp.float32),
            pltpu.VMEM((rows, lanes), jnp.float32),
            pltpu.VMEM((tp_count, rows, lanes), jnp.float32),
            pltpu.SemaphoreType.DMA((1, seq_count)),
            pltpu.SemaphoreType.DMA((1, seq_count)),
            pltpu.SemaphoreType.DMA((1, tp_count)),
            pltpu.SemaphoreType.DMA((1, tp_count)),
        ],
        compiler_params=pltpu.CompilerParams(collective_id=1, has_side_effects=True),
    )(part)


def grads_kernel(
    seq_count,
    tp_count,
    feat_ref,
    small_ref,
    feat_out,
    small_out,
    feat1,
    small1,
    feat_mid,
    small_mid,
    feat2,
    small2,
    small3,
    send1,
    recv1,
    send2,
    recv2,
    send3,
    recv3,
):
    seq_me = lax.axis_index("seq")
    tp_me = lax.axis_index("tensor")
    greet(seq_count, tp_count)
    sources = [lambda p: feat_ref.at[p], lambda p: small_ref.at[p]]
    copies = push("seq", seq_count, sources, [feat1, small1], send1, recv1)
    small1[0] = small_ref[seq_me]
    for copy in copies:
        copy.wait()
    small_mid[...] = ordered_sum("seq", seq_count, small1)

    def body(i, carry):
        total = feat_ref[seq_me, i].astype(jnp.float32)
        for k in range(1, seq_count):
            total = total + feat1[k, i].astype(jnp.float32)
        feat_mid[i] = total
        return carry

    lax.fori_loop(0, tp_count, body, 0)
    sources = [lambda p: feat_mid.at[p], lambda p: small_mid]
    copies = push("tensor", tp_count, sources, [feat2, small2], send2, recv2)
    small2[0] = small_mid[...]
    for copy in copies:
        copy.wait()
    total = feat_mid[tp_me]
    for k in range(1, tp_count):
        total = total + feat2[k]
    feat_out[...] = total
    small3[0] = ordered_sum("tensor", tp_count, small2)
    copies = push("seq", seq_count, [lambda p: small3.at[0]], [small3], send3, recv3)
    for copy in copies:
        copy.wait()
    for origin in range(seq_count):
        small_out[origin] = small3[lax.rem(seq_me - origin + seq_count, seq_count)]


def reduce_grads(feat, small, seq_count, tp_count):
    rows, width = feat.shape[2:]
    extra = small.shape[1]
    vmem = pl.BlockSpec(memory_space=pltpu.VMEM)
    dma = pltpu.SemaphoreType.DMA
    f32 = jnp.float32
    return pl.pallas_call(
        functools.partial(grads_kernel, seq_count, tp_count),
        out_shape=(
            jax.ShapeDtypeStruct((rows, width), f32),
            jax.ShapeDtypeStruct((seq_count, extra, width), f32),
        ),
        in_specs=[vmem, vmem],
        out_specs=(vmem, vmem),
        scratch_shapes=[
            pltpu.VMEM((seq_count, tp_count, rows, width), feat.dtype),
            pltpu.VMEM((seq_count, extra, width), f32),
            pltpu.VMEM((tp_count, rows, width), f32),
            pltpu.VMEM((extra, width), f32),
            pltpu.VMEM((tp_count, rows, width), f32),
            pltpu.VMEM((tp_count, extra, width), f32),
            pltpu.VMEM((seq_count, extra, width), f32),
            dma((2, seq_count)),
            dma((2, seq_count)),
            dma((2, tp_count)),
            dma((2, tp_count)),
            dma((1, seq_count)),
            dma((1, seq_count)),
        ],
        compiler_params=pltpu.CompilerParams(
            collective_id=2, has_side_effects=True, vmem_limit_bytes=32 * 1024 * 1024
        ),
    )(feat, small)


def shards(
    hidden,
    norm_gain,
    query_weight,
    key_weight,
    value_weight,
    output_weight,
    final_gain,
    reward_weight,
    token_ids,
    index_samples,
    feat_weight,
    index_weight,
    first_bias,
    middle_weight,
    second_bias,
    head_weight,
    pair_ids,
):
    highest = lax.Precision.HIGHEST
    tp_count = lax.axis_size("tensor")
    seq_count = lax.axis_size("seq")
    tp_index = lax.axis_index("tensor")
    seq_index = lax.axis_index("seq")
    tok_seq, part_width = hidden.shape
    width = part_width * tp_count
    local_resp = tok_seq // RESP_LEN
    tok_epi = tok_seq // tp_count

    half_dim = HEAD_DIM // 2
    positions = jnp.arange(RESP_LEN, dtype=jnp.int32)
    freqs = rope_base ** (-(jnp.arange(half_dim, dtype=jnp.float32) * 2.0) / HEAD_DIM)
    angles = positions.astype(jnp.float32)[:, None] * freqs[None, :]
    cosine = jnp.cos(angles)
    sine = jnp.sin(angles)

    gain_parts = norm_gain.reshape(tp_count, part_width)
    partials = []
    first_row = tp_index * tok_epi
    own_row = lax.rem(first_row, RESP_LEN)
    own_resp = first_row // RESP_LEN
    own = None
    for r in range(local_resp):
        x = lax.all_gather(hidden[r * RESP_LEN : (r + 1) * RESP_LEN], "tensor", axis=0)
        attended = attend(
            x, gain_parts, query_weight, key_weight, value_weight, cosine, sine
        )
        partials.append(
            jnp.dot(attended, output_weight, preferred_element_type=jnp.float32).astype(
                jnp.bfloat16
            )
        )
        rows = lax.dynamic_slice_in_dim(x, own_row, tok_epi, 1)
        own = rows if own is None else jnp.where(own_resp == r, rows, own)
    residual = jnp.swapaxes(own, 0, 1).reshape(tok_epi, width).astype(jnp.float32)
    partial_out = jnp.concatenate(partials, axis=0)
    mixed = lax.psum_scatter(partial_out, "tensor", scatter_dimension=0, tiled=True)
    summed = residual + mixed.astype(jnp.float32)
    mean_square = jnp.mean(summed * summed, axis=-1, keepdims=True)
    features = (summed * lax.rsqrt(mean_square + norm_eps) * (1.0 + final_gain)).astype(
        jnp.bfloat16
    )

    feat32 = features.astype(jnp.float32)
    base = jnp.dot(feat32, reward_weight, precision=highest)
    feat_part = jnp.dot(feat32, feat_weight, precision=highest)
    index_part = jnp.einsum("sit,ie->ste", index_samples, index_weight, precision=highest)
    first_pre = feat_part[None, :, :] + index_part + first_bias
    first_act = gelu_tanh(first_pre)
    second_pre = (
        jnp.einsum("ste,ef->stf", first_act, middle_weight, precision=highest) + second_bias
    )
    second_act = gelu_tanh(second_pre)
    head_out = jnp.einsum("ste,ei->sti", second_act, head_weight, precision=highest)
    epinet_out = jnp.einsum("sti,sit->st", head_out, index_samples, precision=highest)
    resp_total = 2 * pair_ids.shape[0]
    sample_count = index_samples.shape[0]
    owner = (seq_index * tok_seq + first_row) // RESP_LEN
    slot_ids = jnp.arange(resp_total, dtype=jnp.int32)
    owner_row = (owner == slot_ids).astype(jnp.float32)
    valid = (token_ids != 0).astype(jnp.float32)
    own_total = jnp.sum((base[None, :] + epinet_out) * valid[None, :], axis=1)
    own_count = jnp.sum(valid)
    part = jnp.concatenate([own_total, jnp.full((8,), 0.0, jnp.float32) + own_count])
    part = part[:, None] * owner_row[None, :]
    part = jnp.pad(part, ((0, 0), (0, 128 - resp_total)))
    sums = sum_everywhere(part, seq_count, tp_count)
    totals = sums[:sample_count, :resp_total]
    counts = sums[sample_count, :resp_total]
    means = totals / counts[None, :]
    sign_table = (pair_ids[:, 0:1] == slot_ids[None, :]).astype(jnp.float32) - (
        pair_ids[:, 1:2] == slot_ids[None, :]
    ).astype(jnp.float32)
    margin = jnp.dot(means, sign_table.T, precision=highest)
    pair_margin = margin.T
    margin_grad = -jax.nn.sigmoid(-margin)
    mean_grad = jnp.dot(margin_grad, sign_table, precision=highest) / counts[None, :]
    own_grad = jnp.sum(mean_grad * owner_row[None, :], axis=1)
    reward_grad = own_grad[:, None] * valid[None, :]
    out_grad = jnp.einsum("st,sit->sti", reward_grad, index_samples)
    grad_head = jnp.einsum("ste,sti->ie", second_act, out_grad, precision=highest)
    second_grad = jnp.einsum(
        "sti,ei->ste", out_grad, head_weight, precision=highest
    ) * gelu_slope(second_pre)
    grad_second = jnp.sum(second_grad, axis=(0, 1))
    grad_middle = jnp.einsum("ste,stf->ef", first_act, second_grad, precision=highest)
    first_grad = jnp.einsum(
        "stf,ef->ste", second_grad, middle_weight, precision=highest
    ) * gelu_slope(first_pre)
    grad_first = jnp.sum(first_grad, axis=(0, 1))
    grad_index = jnp.einsum("sit,ste->ie", index_samples, first_grad, precision=highest)
    feat_grad = jnp.sum(first_grad, axis=0)
    grad_feature = jnp.einsum("td,te->de", feat32, feat_grad, precision=highest)

    hidden_units = middle_weight.shape[0]
    index_dim = index_weight.shape[0]
    small = jnp.concatenate(
        [grad_middle, grad_index, grad_head, grad_first[None, :], grad_second[None, :]], axis=0
    )
    used = small.shape[0]
    unit = 8 * seq_count
    padded = (used + unit - 1) // unit * unit
    small = jnp.pad(small, ((0, padded - used), (0, 0)))
    small = small.reshape(seq_count, padded // seq_count, hidden_units)
    feat_blocks = grad_feature.astype(jnp.bfloat16).reshape(
        seq_count, tp_count, width // (seq_count * tp_count), hidden_units
    )
    grad_feature, small = reduce_grads(feat_blocks, small, seq_count, tp_count)
    small = small.reshape(padded, hidden_units)
    at = hidden_units
    return (
        features,
        pair_margin,
        grad_feature,
        small[at : at + index_dim],
        small[at + 2 * index_dim],
        small[:at],
        small[at + 2 * index_dim + 1],
        small[at + index_dim : at + 2 * index_dim].T,
    )


def solution(mesh):
    return jax.shard_map(
        shards,
        mesh=mesh,
        in_specs=(
            P("seq", "tensor"),
            P(),
            P(None, "tensor"),
            P(None, "tensor"),
            P(None, "tensor"),
            P("tensor", None),
            P(),
            P(),
            P(("seq", "tensor")),
            P(None, None, ("seq", "tensor")),
            P(),
            P(),
            P(),
            P(),
            P(),
            P(),
            P(),
        ),
        out_specs=(
            P(("seq", "tensor"), None),
            P(),
            P(("seq", "tensor"), None),
            P(),
            P(),
            P(),
            P(),
            P(),
        ),
        check_vma=False,
    )
```

time: 806 us -> 397 us (0.49); the launches traced: 794 us -> 393 us
  waiting for transfers between devices: 536 us -> 202 us
  blocking collectives: 91.5 us -> 0 us
  Pallas kernels: 0 us -> 88.6 us
  matrix products: 90.4 us -> 50 us
  other arithmetic: 22 us -> 13.3 us
    reduce_scatter x2 -> x1, waiting for transfers between devices: 319 us -> 99.1 us  [shards(): lax.psum_scatter(partial_out, 'tensor', scatter_dimension=0, tiled=True)]
    psum x3 -> x0, blocking collectives: 91.5 us -> none  [the longest x1 44.3 us: shards(): totals, counts = lax.psum((part_totals, part_counts), ('seq', 'tensor'))]
    pallas_call x0 -> x4, Pallas kernels: none -> 88.6 us  [the longest x1 43.7 us: reduce_grads(): pl.pallas_call(functools.partial(grads_kernel, seq_count, tp_count), out_...]
    psum x1 -> x0, waiting for transfers between devices: 73.4 us -> none  [shards(): lax.psum((grad_index, grad_first, grad_middle, grad_second, grad_head), (...]
    dot_general x20 -> x12, matrix products: 75.6 us -> 37.4 us  [the longest x1 12.9 us: shards(): jnp.einsum('sti,ei->ste', out_grad, head_weight, precision=highest)]
    all_to_all x1 -> x0, waiting for transfers between devices: 31.1 us -> none  [shards(): lax.all_to_all(local_feat, 'tensor', split_axis=0, concat_axis=1, tiled=T...]
    reshape x3 -> x1, local copies, waits for them, and re-layouts: 16.2 us -> 0.01 us  [shards(): gain_parts = norm_gain.reshape(tp_count, part_width)]
    all_gather x1 -> x2, waiting for transfers between devices: 112 us -> 102 us  [shards(): lax.all_gather(hidden[r * RESP_LEN:(r + 1) * RESP_LEN], 'tensor', axis=0)]
  transfers between devices with their start and end apart: 5 -> 3, of which waited for: 5 -> 3; matrix products, arithmetic and copies ran while one was open for 2% -> 4% of each run, Pallas kernels for 0% -> 4%
where the time goes in v1:
time: 397 us; the launch traced here: 393 us
  waiting for transfers between devices  202 us (51%)
  Pallas kernels  88.6 us (22%)
  matrix products  50 us (13%)
  local copies, waits for them, and re-layouts  24.9 us (6%)
  between operations  14.4 us (4%)
  other arithmetic  13.3 us (3%)
    all_gather x2, waiting for transfers between devices, shards(): lax.all_gather(hidden[r * RESP_LEN:(r + 1) * RESP_LEN], 'tensor', axis=0)  102 us
    reduce_scatter x1, waiting for transfers between devices, shards(): lax.psum_scatter(partial_out, 'tensor', scatter_dimension=0, tiled=True)  99.1 us
    pallas_call x1, Pallas kernels, reduce_grads(): pl.pallas_call(functools.partial(grads_kernel, seq_count, tp_count), out_...  43.7 us
    pallas_call x2, Pallas kernels, attend(): pl.pallas_call(attention_kernel, grid=(heads,), out_shape=jax.ShapeDtypeS...  34.6 us
    dot_general x1, matrix products, shards(): jnp.einsum('sti,ei->ste', out_grad, head_weight, precision=highest)  12.9 us
    pallas_call x1, Pallas kernels, sum_everywhere(): pl.pallas_call(functools.partial(totals_kernel, seq_count, tp_count), out...  10.2 us
    dot_general x2, matrix products, shards(): jnp.dot(attended, output_weight, preferred_element_type=jnp.float32)  10.1 us
    unnamed x56, local copies, waits for them, and re-layouts  9.43 us
  transfers between devices with their start and end apart: 3, of which 3 were waited for; matrix products, arithmetic and copies ran while one was open for 4% of the time, Pallas kernels for 4%

profile of v1, /device:TPU:9, one launch (start us, length us, event | category | flops | bytes accessed | tf_op | source)
XLA Modules:
  0.0 393.3 jit_solution(14973168209403976839)
XLA Ops:
  7.2 2.8 fusion.61
  10.9 1.8 multiply_sine_fusion
  12.7 59.8 %all-gather.5.cloned.1.call-done = bf16[2048,768]{1,0:T(8,128)(2,1)} async-done(((bf16[512,768]{1,0:T(8,128)(2,1)}), bf16[2048,768]{1,0:T(8,128)(2,1)}) %all-gather.5.cloned.1.call-update) | async-done | bytes 3145744 | tf_op jit(solution)/shard_map/all_gather | solution.py:325
  72.4 1.9 copy-done.1
  74.3 0.9 copy-done.3
  75.3 17.2 %shard_map.225 = bf16[512,1024]{1,0:T(8,128)(2,1)S(1)} custom-call(bf16[4,512,768]{2,1,0:T(8,128)(2,1)S(1)} %bitcast.75, f32[4,768]{1,0:T(4,128)S(1)} %reshape.63.gain_ref, bf16[3072,1024]{1,0:T(8,128)(2,1)} %wq_ref.3, bf16[3072,1024]{1,0:T(8,128)(2,1)} %wk_ref.3, bf16[3072,1024]{1,0:T(8,128)(2,1)} %wv_ref.3, f32[512,128]{1,0:T(8,128)S(1)} %copy-done.3, ...), custom_call_target="tpu_custom_call" | custom-call | flops 10737418240 | bytes 22020096 | tf_op jit(solution)/shard_map/pallas_call | solution.py:92
  92.5 1.0 copy-done.5
  93.5 42.7 %all-gather.7.cloned.1.call-done = bf16[2048,768]{1,0:T(8,128)(2,1)} async-done(((bf16[512,768]{1,0:T(8,128)(2,1)}), bf16[2048,768]{1,0:T(8,128)(2,1)}) %all-gather.7.cloned.1.call-update) | async-done | bytes 3145744 | tf_op jit(solution)/shard_map/all_gather | solution.py:325
  136.2 1.9 copy-done.2
  139.0 17.4 %shard_map.224 = bf16[512,1024]{1,0:T(8,128)(2,1)S(1)} custom-call(bf16[4,512,768]{2,1,0:T(8,128)(2,1)S(1)} %bitcast.77, f32[4,768]{1,0:T(4,128)S(1)} %reshape.63.gain_ref, bf16[3072,1024]{1,0:T(8,128)(2,1)} %wq_ref.3, bf16[3072,1024]{1,0:T(8,128)(2,1)} %wk_ref.3, bf16[3072,1024]{1,0:T(8,128)(2,1)} %wv_ref.3, f32[512,128]{1,0:T(8,128)S(1)} %copy-done.4, ...), custom_call_target="tpu_custom_call" | custom-call | flops 10737418240 | bytes 22020096 | tf_op jit(solution)/shard_map/pallas_call | solution.py:92
  156.4 3.7 convolution_convert_fusion
  160.1 6.4 %convolution_convert_fusion.1 = bf16[512,3072]{1,0:T(8,128)(2,1)S(1)} fusion(bf16[512,1024]{1,0:T(8,128)(2,1)S(1)} %shard_map.224, bf16[1024,3072]{1,0:T(8,128)(2,1)} %param.22), kind=kOutput, calls=%fused_computation.2 | convolution fusion | flops 3222798336 | bytes 10485760 | tf_op jit(solution)/shard_map/dot_general | solution.py:330
  166.5 3.1 pad_maximum_fusion
  171.0 3.9 convert_bitcast_fusion
  174.9 4.0 %copy.27 = f32[256,4,768]{0,2,1:T(8,128)} copy(f32[256,4,768]{2,0,1:T(8,128)} %convert_bitcast_fusion) | data formatting | bytes 6291456 | tf_op jit(solution)/shard_map/convert_element_type | solution.py:336
  178.8 3.8 copy.28
  182.6 99.1 %reduce-scatter.2.cloned.1.call-done = bf16[256,3072]{1,0:T(8,128)(2,1)} async-done(((bf16[1024,3072]{1,0:T(8,128)(2,1)}), bf16[256,3072]{1,0:T(8,128)(2,1)}) %reduce-scatter.2.cloned.1.call-update) | async-done | bytes 1572880 | tf_op jit(solution)/shard_map/reduce_scatter | solution.py:338
  281.7 3.0 multiply_reduce_fusion
  286.2 1.8 fusion.65
  288.0 1.3 fusion.64
  289.3 2.0 add_add_fusion
  291.3 2.2 fusion.17
  293.6 2.5 fusion.14
  297.6 10.2 %shard_map.226 = f32[16,128]{1,0:T(8,128)} custom-call(f32[16,128]{1,0:T(8,128)} %pad.9.part_ref), custom_call_target="tpu_custom_call" | custom-call | tf_op jit(solution)/shard_map/pallas_call | solution.py:173
  309.8 3.3 convolution_bitcast_fusion.1
  313.1 12.9 %fusion.63 = (f32[256]{0:T(256)S(1)}, f32[8,256,256]{2,1,0:T(8,128)S(1)}) fusion(f32[8,256,256]{2,1,0:T(8,128)S(1)} %copy-done.26, f32[256]{0:T(256)S(1)} %copy-done.24, f32[256,8]{0,1:T(8,128)S(1)} %copy-done.23, f32[8,8,256]{2,1,0:T(8,128)S(1)} %copy-done.12, f32[8,256]{1,0:T(8,128)S(1)} %broadcast_multiply_fusion), kind=kOutput, calls=%fused_computation.101 | convolution fusion | flops 60833536 | bytes 4278272 | tf_op jit(solution)/shard_map/sti,ei->ste/dot_general | solution.py:383
  326.0 4.6 %convolution_bitcast_fusion = f32[256,256]{1,0:T(8,128)} fusion(f32[8,256,256]{2,1,0:T(8,128)S(1)} %get-tuple-element.42, f32[8,256,256]{2,1,0:T(8,128)S(1)} %copy-done.11), kind=kOutput, calls=%fused_computation.29 | convolution fusion | flops 1614807040 | bytes 4456448 | tf_op jit(solution)/shard_map/ste,stf->ef/dot_general | solution.py:387
  330.7 3.7 fusion.60
  334.4 1.1 convolution_bitcast_fusion.2
  335.5 1.0 concatenate.11
  336.5 3.2 convolution_convert_fusion.2
  339.8 43.7 %shard_map.227 = (f32[96,256]{1,0:T(8,128)S(1)}, f32[8,40,256]{2,1,0:T(8,128)S(1)}) custom-call(bf16[8,4,96,256]{3,2,1,0:T(8,128)(2,1)S(1)} %bitcast.72, f32[8,40,256]{2,1,0:T(8,128)S(1)} %bitcast.73), custom_call_target="tpu_custom_call" | custom-call | tf_op jit(solution)/shard_map/pallas_call | solution.py:253
  (80 shorter events, 11.1 us)
Async XLA Ops:
  7.2 278.9 %copy-start = (f32[3072,256]{1,0:T(8,128)S(1)}, f32[3072,256]{1,0:T(8,128)}, u32[]{:S(2)}) copy-start(f32[3072,256]{1,0:T(8,128)} %param.27) | copy-start | bytes 9437188
  7.2 3.7 copy-start.14
  7.2 65.2 %all-gather.5.cloned.1.call-start = ((), (), s32[]{:S(2)}) async-start(), calls=%async_computation.2 | async-start | bytes 3932160 | tf_op jit(solution)/shard_map/all_gather | solution.py:325
  10.0 126.1 %all-gather.7.cloned.1.call-start = ((), (), s32[]{:S(2)}) async-start(), calls=%async_computation.3 | async-start | bytes 3932160 | tf_op jit(solution)/shard_map/all_gather | solution.py:325
  10.8 270.9 %reduce-scatter.2.cloned.1.call-start = ((), (), s32[]{:S(2)}) async-start(), calls=%async_computation.1 | async-start | bytes 7864320 | tf_op jit(solution)/shard_map/reduce_scatter | solution.py:338
  72.4 1.9 copy-start.1
  74.3 0.9 copy-start.3
  92.5 1.0 copy-start.5
  136.2 1.9 copy-start.2
  138.1 0.9 copy-start.4
  139.0 17.4 %copy-start.6 = (bf16[512,1024]{1,0:T(8,128)(2,1)S(1)}, bf16[512,1024]{1,0:T(8,128)(2,1)}, u32[]{:S(2)}) copy-start(bf16[512,1024]{1,0:T(8,128)(2,1)} %copy-done.5) | copy-start | bytes 3145732
  139.0 17.4 %copy-start.20 = (bf16[1024,3072]{1,0:T(8,128)(2,1)S(1)}, bf16[1024,3072]{1,0:T(8,128)(2,1)}, u32[]{:S(2)}) copy-start(bf16[1024,3072]{1,0:T(8,128)(2,1)} %param.22) | copy-start | bytes 18874372
  169.6 0.7 copy-start.18
  169.6 1.3 copy-start.19
  169.6 1.3 copy-start.15
  281.7 3.3 copy-start.7
  281.7 3.8 copy-start.9
  286.1 1.8 copy-start.8
  286.1 1.8 copy-start.13
  286.1 3.1 copy-start.12
  286.1 3.2 copy-start.16
  286.1 3.2 copy-start.17
  287.9 3.4 copy-start.21
  291.3 2.3 copy-start.10
  291.3 2.3 copy-start.23
  291.3 2.3 copy-start.24
  293.6 2.6 copy-start.25
  309.8 3.3 copy-start.26
  313.1 12.9 %copy-start.11 = (f32[8,256,256]{2,1,0:T(8,128)S(1)}, f32[8,256,256]{2,1,0:T(8,128)}, u32[]{:S(2)}) copy-start(f32[8,256,256]{2,1,0:T(8,128)} %copy-done.10) | copy-start | bytes 6291460
  326.0 4.6 %copy-start.22 = (f32[256,256]{1,0:T(8,128)S(1)}, f32[256,256]{1,0:T(8,128)}, u32[]{:S(2)}) copy-start(f32[256,256]{1,0:T(8,128)} %param.30) | copy-start | bytes 786436
Sparse Core Ops, SparseCore 0:
  10.2 62.2 all-gather.4
  74.0 62.1 all-gather.6
  169.8 111.8 reduce-scatter.1

commit v2 on v1

--- a/solution.py
+++ b/solution.py
@@ -298,7 +298,7 @@
     head_weight,
     pair_ids,
 ):
-    highest = lax.Precision.HIGHEST
+    precise = lax.Precision.HIGH
     tp_count = lax.axis_size("tensor")
     seq_count = lax.axis_size("seq")
     tp_index = lax.axis_index("tensor")
@@ -315,55 +315,91 @@
     cosine = jnp.cos(angles)
     sine = jnp.sin(angles)
 
+    share = RESP_LEN // tp_count
+    group = tp_count // local_resp
+    there = [
+        [(t, ((t + p) % local_resp) * group + t // local_resp) for t in range(tp_count)]
+        for p in range(local_resp)
+    ]
+    back = [[(d, t) for t, d in pairs] for pairs in there]
+
+    def piece_of(p):
+        return lax.rem(tp_index + p, local_resp)
+
+    def slot_of(p):
+        return lax.rem(tp_index // group - p + local_resp, local_resp)
+
+    valid_here = (token_ids != 0).astype(jnp.float32)
+    sample_count, index_dim, _ = index_samples.shape
+    lanes = jnp.concatenate(
+        [index_samples.reshape(sample_count * index_dim, tok_epi), valid_here[None, :]], axis=0
+    )
+    lanes = jnp.swapaxes(lanes.reshape(lanes.shape[0], local_resp, share), 0, 1)
+    moved = jnp.zeros_like(lanes)
+    for p in range(local_resp):
+        sent = lax.dynamic_index_in_dim(lanes, slot_of(p), 0, keepdims=False)
+        got = lax.ppermute(sent, "tensor", back[p])
+        moved = lax.dynamic_update_index_in_dim(moved, got, piece_of(p), 0)
+    rows_n = sample_count * tok_epi
+    z = (
+        moved[:, : sample_count * index_dim]
+        .reshape(local_resp, sample_count, index_dim, share)
+        .transpose(1, 0, 3, 2)
+        .reshape(rows_n, index_dim)
+    )
+    valid = moved[:, sample_count * index_dim]
+
     gain_parts = norm_gain.reshape(tp_count, part_width)
-    partials = []
-    first_row = tp_index * tok_epi
-    own_row = lax.rem(first_row, RESP_LEN)
-    own_resp = first_row // RESP_LEN
-    own = None
+    pieces = []
     for r in range(local_resp):
         x = lax.all_gather(hidden[r * RESP_LEN : (r + 1) * RESP_LEN], "tensor", axis=0)
         attended = attend(
             x, gain_parts, query_weight, key_weight, value_weight, cosine, sine
         )
-        partials.append(
-            jnp.dot(attended, output_weight, preferred_element_type=jnp.float32).astype(
-                jnp.bfloat16
-            )
+        partial = jnp.dot(attended, output_weight, preferred_element_type=jnp.float32).astype(
+            jnp.bfloat16
         )
-        rows = lax.dynamic_slice_in_dim(x, own_row, tok_epi, 1)
-        own = rows if own is None else jnp.where(own_resp == r, rows, own)
-    residual = jnp.swapaxes(own, 0, 1).reshape(tok_epi, width).astype(jnp.float32)
-    partial_out = jnp.concatenate(partials, axis=0)
-    mixed = lax.psum_scatter(partial_out, "tensor", scatter_dimension=0, tiled=True)
-    summed = residual + mixed.astype(jnp.float32)
-    mean_square = jnp.mean(summed * summed, axis=-1, keepdims=True)
-    features = (summed * lax.rsqrt(mean_square + norm_eps) * (1.0 + final_gain)).astype(
-        jnp.bfloat16
-    )
-
-    feat32 = features.astype(jnp.float32)
-    base = jnp.dot(feat32, reward_weight, precision=highest)
-    feat_part = jnp.dot(feat32, feat_weight, precision=highest)
-    index_part = jnp.einsum("sit,ie->ste", index_samples, index_weight, precision=highest)
-    first_pre = feat_part[None, :, :] + index_part + first_bias
+        mixed = lax.psum_scatter(partial, "tensor", scatter_dimension=0, tiled=True)
+        own = lax.dynamic_slice_in_dim(x, tp_index * share, share, 1)
+        residual = jnp.swapaxes(own, 0, 1).reshape(share, width).astype(jnp.float32)
+        summed = residual + mixed.astype(jnp.float32)
+        mean_square = jnp.mean(summed * summed, axis=-1, keepdims=True)
+        pieces.append(
+            (summed * lax.rsqrt(mean_square + norm_eps) * (1.0 + final_gain)).astype(jnp.bfloat16)
+        )
+    held = jnp.stack(pieces, axis=0)
+    features = jnp.zeros_like(held)
+    for p in range(local_resp):
+        sent = lax.dynamic_index_in_dim(held, piece_of(p), 0, keepdims=False)
+        got = lax.ppermute(sent, "tensor", there[p])
+        features = lax.dynamic_update_index_in_dim(features, got, slot_of(p), 0)
+    features = features.reshape(tok_epi, width)
+
+    feat32 = held.reshape(tok_epi, width).astype(jnp.float32)
+    hidden_units = middle_weight.shape[0]
+    base = jnp.sum(feat32 * reward_weight, axis=1)
+    feat_part = jnp.dot(feat32, feat_weight, precision=precise)
+    index_part = jnp.dot(z, index_weight, precision=precise) + first_bias
+    first_pre = (index_part.reshape(sample_count, tok_epi, hidden_units) + feat_part).reshape(
+        rows_n, hidden_units
+    )
     first_act = gelu_tanh(first_pre)
-    second_pre = (
-        jnp.einsum("ste,ef->stf", first_act, middle_weight, precision=highest) + second_bias
-    )
+    second_pre = jnp.dot(first_act, middle_weight, precision=precise) + second_bias
     second_act = gelu_tanh(second_pre)
-    head_out = jnp.einsum("ste,ei->sti", second_act, head_weight, precision=highest)
-    epinet_out = jnp.einsum("sti,sit->st", head_out, index_samples, precision=highest)
+    head_rows = jnp.dot(z, head_weight.T, precision=precise)
+    epinet_out = jnp.sum(second_act * head_rows, axis=1).reshape(
+        sample_count, local_resp, share
+    )
     resp_total = 2 * pair_ids.shape[0]
-    sample_count = index_samples.shape[0]
-    owner = (seq_index * tok_seq + first_row) // RESP_LEN
+    owner = seq_index * local_resp + jnp.arange(local_resp, dtype=jnp.int32)
     slot_ids = jnp.arange(resp_total, dtype=jnp.int32)
-    owner_row = (owner == slot_ids).astype(jnp.float32)
-    valid = (token_ids != 0).astype(jnp.float32)
-    own_total = jnp.sum((base[None, :] + epinet_out) * valid[None, :], axis=1)
-    own_count = jnp.sum(valid)
-    part = jnp.concatenate([own_total, jnp.full((8,), 0.0, jnp.float32) + own_count])
-    part = part[:, None] * owner_row[None, :]
+    owner_table = (owner[:, None] == slot_ids[None, :]).astype(jnp.float32)
+    own_totals = jnp.sum(
+        (base.reshape(local_resp, share)[None] + epinet_out) * valid[None], axis=2
+    )
+    own_counts = jnp.zeros((8, local_resp), jnp.float32) + jnp.sum(valid, axis=1)
+    part = jnp.concatenate([own_totals, own_counts], axis=0)
+    part = jnp.sum(part[:, :, None] * owner_table[None], axis=1)
     part = jnp.pad(part, ((0, 0), (0, 128 - resp_total)))
     sums = sum_everywhere(part, seq_count, tp_count)
     totals = sums[:sample_count, :resp_total]
@@ -372,29 +408,23 @@
     sign_table = (pair_ids[:, 0:1] == slot_ids[None, :]).astype(jnp.float32) - (
         pair_ids[:, 1:2] == slot_ids[None, :]
     ).astype(jnp.float32)
-    margin = jnp.dot(means, sign_table.T, precision=highest)
+    margin = jnp.dot(means, sign_table.T, precision=lax.Precision.HIGHEST)
     pair_margin = margin.T
     margin_grad = -jax.nn.sigmoid(-margin)
-    mean_grad = jnp.dot(margin_grad, sign_table, precision=highest) / counts[None, :]
-    own_grad = jnp.sum(mean_grad * owner_row[None, :], axis=1)
-    reward_grad = own_grad[:, None] * valid[None, :]
-    out_grad = jnp.einsum("st,sit->sti", reward_grad, index_samples)
-    grad_head = jnp.einsum("ste,sti->ie", second_act, out_grad, precision=highest)
-    second_grad = jnp.einsum(
-        "sti,ei->ste", out_grad, head_weight, precision=highest
-    ) * gelu_slope(second_pre)
-    grad_second = jnp.sum(second_grad, axis=(0, 1))
-    grad_middle = jnp.einsum("ste,stf->ef", first_act, second_grad, precision=highest)
-    first_grad = jnp.einsum(
-        "stf,ef->ste", second_grad, middle_weight, precision=highest
-    ) * gelu_slope(first_pre)
-    grad_first = jnp.sum(first_grad, axis=(0, 1))
-    grad_index = jnp.einsum("sit,ste->ie", index_samples, first_grad, precision=highest)
-    feat_grad = jnp.sum(first_grad, axis=0)
-    grad_feature = jnp.einsum("td,te->de", feat32, feat_grad, precision=highest)
-
-    hidden_units = middle_weight.shape[0]
-    index_dim = index_weight.shape[0]
+    mean_grad = jnp.dot(margin_grad, sign_table, precision=lax.Precision.HIGHEST) / counts[None, :]
+    own_grad = jnp.sum(mean_grad[:, None, :] * owner_table[None], axis=2)
+    scale = (own_grad[:, :, None] * valid[None]).reshape(rows_n, 1)
+    rows_dims = (((0,), (0,)), ((), ()))
+    grad_head = lax.dot_general(z * scale, second_act, rows_dims, precision=precise)
+    second_grad = scale * head_rows * gelu_slope(second_pre)
+    grad_second = jnp.sum(second_grad, axis=0)
+    grad_middle = lax.dot_general(first_act, second_grad, rows_dims, precision=precise)
+    first_grad = jnp.dot(second_grad, middle_weight.T, precision=precise) * gelu_slope(first_pre)
+    grad_first = jnp.sum(first_grad, axis=0)
+    grad_index = lax.dot_general(z, first_grad, rows_dims, precision=precise)
+    feat_grad = jnp.sum(first_grad.reshape(sample_count, tok_epi, hidden_units), axis=0)
+    grad_feature = lax.dot_general(feat32, feat_grad, rows_dims, precision=precise)
+
     small = jnp.concatenate(
         [grad_middle, grad_index, grad_head, grad_first[None, :], grad_second[None, :]], axis=0
     )

time: 397 us -> 376 us (0.947)
  waiting for transfers between devices: 202 us -> 174 us
  matrix products: 50 us -> 30.6 us
  starting transfers between devices: 0.12 us -> 12.9 us
  local copies, waits for them, and re-layouts: 24.9 us -> 34.5 us
  other arithmetic: 13.3 us -> 19.8 us
    reduce_scatter x1 -> x2, waiting for transfers between devices: 99.1 us -> 67 us  [shards(): mixed = lax.psum_scatter(partial, 'tensor', scatter_dimension=0, tiled=True)]
    dot_general x12 -> x11, matrix products: 37.4 us -> 18.1 us  [the longest x1 2.86 us: shards(): lax.dot_general(z * scale, second_act, rows_dims, precision=precise)]
    ppermute x0 -> x4, starting transfers between devices: none -> 12.8 us  [the longest x2 8.38 us: shards(): got = lax.ppermute(sent, 'tensor', there[p])]
    ppermute x0 -> x4, waiting for transfers between devices: none -> 7.13 us  [the longest x2 7.13 us: shards(): got = lax.ppermute(sent, 'tensor', back[p])]
    convert_element_type x2 -> x4, local copies, waits for them, and re-layouts: 7.79 us -> 12.2 us  [shards(): residual = jnp.swapaxes(own, 0, 1).reshape(share, width).astype(jnp.float32)]
    reduce_sum x2 -> x6, other arithmetic: 0.72 us -> 4.82 us  [the longest x1 2.46 us: shards(): jnp.sum(first_grad.reshape(sample_count, tok_epi, hidden_units), axis=0)]
    unnamed x56 -> x71, local copies, waits for them, and re-layouts: 9.43 us -> 9.82 us
  transfers between devices with their start and end apart: 3 -> 8, of which waited for: 3 -> 6; matrix products, arithmetic and copies ran while one was open for 4% -> 13% of each run, Pallas kernels for 4% -> 21%
where the time goes in v2:
time: 376 us; the launch traced here: 375 us
  waiting for transfers between devices  174 us (46%)
  Pallas kernels  88.8 us (24%)
  local copies, waits for them, and re-layouts  34.5 us (9%)
  matrix products  30.6 us (8%)
  other arithmetic  19.8 us (5%)
  between operations  14.4 us (4%)
  starting transfers between devices  12.9 us (3%)
    all_gather x2, waiting for transfers between devices, shards(): lax.all_gather(hidden[r * RESP_LEN:(r + 1) * RESP_LEN], 'tensor', axis=0)  98.9 us
    reduce_scatter x2, waiting for transfers between devices, shards(): mixed = lax.psum_scatter(partial, 'tensor', scatter_dimension=0, tiled=True)  67 us
    pallas_call x1, Pallas kernels, reduce_grads(): pl.pallas_call(functools.partial(grads_kernel, seq_count, tp_count), out_...  44 us
    pallas_call x2, Pallas kernels, attend(): pl.pallas_call(attention_kernel, grid=(heads,), out_shape=jax.ShapeDtypeS...  34.6 us
    dot_general x2, matrix products, shards(): jnp.dot(attended, output_weight, preferred_element_type=jnp.float32)  12.5 us
    convert_element_type x4, local copies, waits for them, and re-layouts, shards(): residual = jnp.swapaxes(own, 0, 1).reshape(share, width).astype(jnp.float32)  12.2 us
    pallas_call x1, Pallas kernels, sum_everywhere(): pl.pallas_call(functools.partial(totals_kernel, seq_count, tp_count), out...  10.2 us
    unnamed x71, local copies, waits for them, and re-layouts  9.82 us
  transfers between devices with their start and end apart: 8, of which 6 were waited for; matrix products, arithmetic and copies ran while one was open for 13% of the time, Pallas kernels for 21%

profile of v2, /device:TPU:9, one launch (start us, length us, event | category | flops | bytes accessed | tf_op | source)
XLA Modules:
  0.0 374.9 jit_solution(10812285037766862237)
XLA Ops:
  7.2 2.8 fusion.56
  12.6 59.8 %all-gather.5.cloned.1.call-done = bf16[2048,768]{1,0:T(8,128)(2,1)} async-done(((bf16[512,768]{1,0:T(8,128)(2,1)}), bf16[2048,768]{1,0:T(8,128)(2,1)}) %all-gather.5.cloned.1.call-update) | async-done | bytes 3145744 | tf_op jit(solution)/shard_map/all_gather | solution.py:355
  75.2 17.4 %shard_map.224 = bf16[512,1024]{1,0:T(8,128)(2,1)S(1)} custom-call(bf16[4,512,768]{2,1,0:T(8,128)(2,1)S(1)} %bitcast.81, f32[4,768]{1,0:T(4,128)S(1)} %reshape.150.gain_ref, bf16[3072,1024]{1,0:T(8,128)(2,1)} %wq_ref.3, bf16[3072,1024]{1,0:T(8,128)(2,1)} %wk_ref.3, bf16[3072,1024]{1,0:T(8,128)(2,1)} %wv_ref.3, f32[512,128]{1,0:T(8,128)S(1)} %copy-done.1, ...), custom_call_target="tpu_custom_call" | custom-call | flops 10737418240 | bytes 22020096 | tf_op jit(solution)/shard_map/pallas_call | solution.py:92
  92.7 4.8 %convolution_convert_fusion.1 = bf16[512,3072]{1,0:T(8,128)(2,1)} fusion(bf16[512,1024]{1,0:T(8,128)(2,1)S(1)} %shard_map.224, bf16[1024,3072]{1,0:T(8,128)(2,1)S(1)} %copy-done.29), kind=kOutput, calls=%fused_computation.1 | convolution fusion | flops 3222798336 | bytes 10485760 | tf_op jit(solution)/shard_map/dot_general | solution.py:359
  97.5 39.2 %all-gather.7.cloned.1.call-done = bf16[2048,768]{1,0:T(8,128)(2,1)} async-done(((bf16[512,768]{1,0:T(8,128)(2,1)}), bf16[2048,768]{1,0:T(8,128)(2,1)}) %all-gather.7.cloned.1.call-update) | async-done | bytes 3145744 | tf_op jit(solution)/shard_map/all_gather | solution.py:355
  139.6 17.2 %shard_map.225 = bf16[512,1024]{1,0:T(8,128)(2,1)S(1)} custom-call(bf16[4,512,768]{2,1,0:T(8,128)(2,1)S(1)} %bitcast.83, f32[4,768]{1,0:T(4,128)S(1)} %reshape.150.gain_ref, bf16[3072,1024]{1,0:T(8,128)(2,1)} %wq_ref.3, bf16[3072,1024]{1,0:T(8,128)(2,1)} %wk_ref.3, bf16[3072,1024]{1,0:T(8,128)(2,1)} %wv_ref.3, f32[512,128]{1,0:T(8,128)S(1)} %copy-done.2, ...), custom_call_target="tpu_custom_call" | custom-call | flops 10737418240 | bytes 22020096 | tf_op jit(solution)/shard_map/pallas_call | solution.py:92
  156.8 7.7 %convolution_convert_fusion = bf16[512,3072]{1,0:T(8,128)(2,1)} fusion(bf16[512,1024]{1,0:T(8,128)(2,1)S(1)} %shard_map.225, bf16[1024,3072]{1,0:T(8,128)(2,1)} %param.22), kind=kOutput, calls=%fused_computation | convolution fusion | flops 3222798336 | bytes 10485760 | tf_op jit(solution)/shard_map/dot_general | solution.py:359
  165.5 4.2 %collective-permute-start.2 = (f32[65,128]{1,0:T(8,128)S(1)}, f32[65,128]{1,0:T(8,128)S(1)}, u32[]{:S(2)}, u32[]{:S(2)}) collective-permute-start(f32[65,128]{1,0:T(8,128)S(1)} %get-tuple-element.73), channel_id=1, source_target_pairs={{0,0},{2,1},{1,2},{3,3},{4,4},{6,5},{5,6},{7,7},{8,8},{10,9},{9,10... | collective-permute-start | bytes 99848 | tf_op jit(solution)/shard_map/ppermute | solution.py:341
  170.0 4.6 %collective-permute-done.2 = f32[65,128]{1,0:T(8,128)S(1)} collective-permute-done((f32[65,128]{1,0:T(8,128)S(1)}, f32[65,128]{1,0:T(8,128)S(1)}, u32[]{:S(2)}, u32[]{:S(2)}) %collective-permute-start.2) | collective-permute-done | bytes 33312 | tf_op jit(solution)/shard_map/ppermute | solution.py:341
  174.6 2.6 collective-permute-done.3
  177.3 2.4 convert_bitcast_fusion.1
  179.7 3.1 copy.53
  182.8 3.0 copy.54
  185.8 2.4 convert_bitcast_fusion
  188.2 3.1 copy.55
  191.3 3.0 copy.56
  194.3 7.2 %reduce-scatter.3.cloned.1.call-done = bf16[128,3072]{1,0:T(8,128)(2,1)} async-done(((bf16[512,3072]{1,0:T(8,128)(2,1)}), bf16[128,3072]{1,0:T(8,128)(2,1)}) %reduce-scatter.3.cloned.1.call-update) | async-done | bytes 786448 | tf_op jit(solution)/shard_map/reduce_scatter | solution.py:362
  201.6 1.9 multiply_reduce_fusion.3
  203.5 59.8 %reduce-scatter.5.cloned.1.call-done = bf16[128,3072]{1,0:T(8,128)(2,1)} async-done(((bf16[512,3072]{1,0:T(8,128)(2,1)}), bf16[128,3072]{1,0:T(8,128)(2,1)}) %reduce-scatter.5.cloned.1.call-update) | async-done | bytes 786448 | tf_op jit(solution)/shard_map/reduce_scatter | solution.py:362
  263.2 2.0 multiply_reduce_fusion.2
  265.6 2.2 fusion.17
  273.3 2.8 multiply_reduce_fusion.1
  277.2 10.2 %shard_map.226 = f32[16,128]{1,0:T(8,128)} custom-call(f32[16,128]{1,0:T(8,128)} %pad.8.part_ref), custom_call_target="tpu_custom_call" | custom-call | tf_op jit(solution)/shard_map/pallas_call | solution.py:173
  289.4 2.9 fusion.15
  294.0 2.2 fusion.59
  296.3 2.2 fusion.14
  300.2 2.9 collective-permute-start
  303.8 2.5 concatenate.21
  307.3 2.5 reduce_sum.107
  309.8 5.5 %collective-permute-start.1 = (bf16[128,3072]{1,0:T(8,128)(2,1)}, bf16[128,3072]{1,0:T(8,128)(2,1)}, u32[]{:S(2)}, u32[]{:S(2)}) collective-permute-start(bf16[128,3072]{1,0:T(8,128)(2,1)} %get-tuple-element.62), channel_id=1, source_target_pairs={{0,2},{1,0},{2,3},{3,1},{4,6},{5,4},{6,7},{7,5},{8,10},{9,8},{10,1... | collective-permute-start | bytes 2359304 | tf_op jit(solution)/shard_map/ppermute | solution.py:374
  315.3 2.8 convolution_convert_fusion.2
  318.1 44.0 %shard_map.227 = (f32[96,256]{1,0:T(8,128)S(1)}, f32[8,40,256]{2,1,0:T(8,128)S(1)}) custom-call(bf16[8,4,96,256]{3,2,1,0:T(8,128)(2,1)S(1)} %bitcast.75, f32[8,40,256]{2,1,0:T(8,128)S(1)} %bitcast.76), custom_call_target="tpu_custom_call" | custom-call | tf_op jit(solution)/shard_map/pallas_call | solution.py:253
  (129 shorter events, 29.8 us)
Async XLA Ops:
  7.2 261.8 %copy-start = (f32[3072,256]{1,0:T(8,128)S(1)}, f32[3072,256]{1,0:T(8,128)}, u32[]{:S(2)}) copy-start(f32[3072,256]{1,0:T(8,128)} %param.27) | copy-start | bytes 9437188
  7.2 3.6 copy-start.23
  7.2 65.2 %all-gather.5.cloned.1.call-start = ((), (), s32[]{:S(2)}) async-start(), calls=%async_computation.4 | async-start | bytes 3932160 | tf_op jit(solution)/shard_map/all_gather | solution.py:355
  10.0 126.7 %all-gather.7.cloned.1.call-start = ((), (), s32[]{:S(2)}) async-start(), calls=%async_computation.5 | async-start | bytes 3932160 | tf_op jit(solution)/shard_map/all_gather | solution.py:355
  10.8 190.8 %reduce-scatter.3.cloned.1.call-start = ((), (), s32[]{:S(2)}) async-start(), calls=%async_computation.2 | async-start | bytes 3932160 | tf_op jit(solution)/shard_map/reduce_scatter | solution.py:362
  73.3 1.9 copy-start.3
  75.2 17.4 %copy-start.29 = (bf16[1024,3072]{1,0:T(8,128)(2,1)S(1)}, bf16[1024,3072]{1,0:T(8,128)(2,1)}, u32[]{:S(2)}) copy-start(bf16[1024,3072]{1,0:T(8,128)(2,1)} %param.22) | copy-start | bytes 18874372
  97.5 165.8 %reduce-scatter.5.cloned.1.call-start = ((), (), s32[]{:S(2)}) async-start(), calls=%async_computation.3 | async-start | bytes 3932160 | tf_op jit(solution)/shard_map/reduce_scatter | solution.py:362
  137.7 1.9 copy-start.4
  164.5 5.4 %copy-start.28 = (s32[8,2]{0,1:T(2,128)S(1)}, s32[8,2]{0,1:T(2,128)}, u32[]{:S(2)}) copy-start(s32[8,2]{0,1:T(2,128)} %param.33) | copy-start | bytes 196
  164.5 5.4 %copy-start.24 = (f32[3072]{0:T(1024)S(1)}, f32[3072]{0:T(1024)}, u32[]{:S(2)}) copy-start(f32[3072]{0:T(1024)} %param.23) | copy-start | bytes 36868
  165.5 9.1 %collective-permute-start.2 = (f32[65,128]{1,0:T(8,128)S(1)}, f32[65,128]{1,0:T(8,128)S(1)}, u32[]{:S(2)}, u32[]{:S(2)}) collective-permute-start(f32[65,128]{1,0:T(8,128)S(1)} %get-tuple-element.73), channel_id=1, source_target_pairs={{0,0},{2,1},{1,2},{3,3},{4,4},{6,5},{5,6},{7,7},{8,8},{10,9},{9,10... | collective-permute-start | bytes 99848 | tf_op jit(solution)/shard_map/ppermute | solution.py:341
  169.6 7.5 %collective-permute-start.3 = (f32[65,128]{1,0:T(8,128)S(1)}, f32[65,128]{1,0:T(8,128)S(1)}, u32[]{:S(2)}, u32[]{:S(2)}) collective-permute-start(f32[65,128]{1,0:T(8,128)S(1)} %get-tuple-element.72), channel_id=1, source_target_pairs={{2,0},{0,1},{3,2},{1,3},{6,4},{4,5},{7,6},{5,7},{10,8},{8,9},{11,1... | collective-permute-start | bytes 99848 | tf_op jit(solution)/shard_map/ppermute | solution.py:341
  263.2 2.1 copy-start.8
  263.2 2.3 copy-start.14
  267.8 1.2 copy-start.9
  268.6 1.4 copy-start.7
  271.8 1.5 copy-start.15
  271.8 1.5 copy-start.32
  273.3 2.8 copy-start.17
  289.4 2.9 copy-start.18
  289.4 2.9 copy-start.19
  292.3 1.7 copy-start.16
  292.3 1.7 copy-start.31
  296.2 6.9 %copy-start.13 = (f32[2048,256]{1,0:T(8,128)}, f32[2048,256]{1,0:T(8,128)S(1)}, u32[]{:S(2)}) copy-start(f32[2048,256]{1,0:T(8,128)S(1)} %get-tuple-element.83) | copy-start | bytes 6291460
  296.3 2.2 copy-start.10
  296.3 2.2 copy-start.12
  300.2 64.4 %collective-permute-start = (bf16[128,3072]{1,0:T(8,128)(2,1)}, bf16[128,3072]{1,0:T(8,128)(2,1)}, u32[]{:S(2)}, u32[]{:S(2)}) collective-permute-start(bf16[128,3072]{1,0:T(8,128)(2,1)} %get-tuple-element.63), channel_id=1, source_target_pairs={{0,0},{1,2},{2,1},{3,3},{4,4},{5,6},{6,5},{7,7},{8,8},{9,10},{10,9... | collective-permute-start | bytes 2359304 | tf_op jit(solution)/shard_map/ppermute | solution.py:374
  309.8 56.2 %collective-permute-start.1 = (bf16[128,3072]{1,0:T(8,128)(2,1)}, bf16[128,3072]{1,0:T(8,128)(2,1)}, u32[]{:S(2)}, u32[]{:S(2)}) collective-permute-start(bf16[128,3072]{1,0:T(8,128)(2,1)} %get-tuple-element.62), channel_id=1, source_target_pairs={{0,2},{1,0},{2,3},{3,1},{4,6},{5,4},{6,7},{7,5},{8,10},{9,8},{10,1... | collective-permute-start | bytes 2359304 | tf_op jit(solution)/shard_map/ppermute | solution.py:374
  362.0 1.9 copy-start.5
  364.6 2.6 copy-start.6
  367.2 1.2 copy-start.20
  (10 other events, 9.1 us)
Sparse Core Ops, SparseCore 0:
  10.1 62.2 all-gather.4
  74.5 62.1 all-gather.6
  139.0 62.4 reduce-scatter.2
  203.7 59.4 reduce-scatter.4
